TPU v7x, 128 devices: a whole 4x4x4 slice. The times are simulated.
128 devices in a mesh: dp: 8 (over z, y_lo), fsdp: 16 (over y_hi, x, core).
Axes of the slice: x: 4, y: 4 (y_hi: 2, y_lo: 2; y = y_hi * 2 + y_lo), z: 4, core: 2. Of those that a mesh axis runs over, the one named last changes fastest.
Arguments:
- hidden: bfloat16 [2048, 32, 5120], P(('dp', 'fsdp')), may hold values from -6 to 6
- queries: bfloat16 [2048, 32, 2560], P(('dp', 'fsdp')), may hold values from -6 to 6
- out_grad: bfloat16 [2048, 32, 2560], P(('dp', 'fsdp')), may hold values from -6 to 6
- counts: int32 [2048], P(('dp', 'fsdp')), may hold values from 1 to 2
- send_peer: int32 [2048], P(('dp', 'fsdp')), may hold values from 0 to 7, as said below
- recv_from: int32 [2048], P(('dp', 'fsdp')), may hold values from 0 to 7, as said below
- key_weight: bfloat16 [5120, 512], P('fsdp'), may hold values from -0.6 to 0.6
- value_weight: bfloat16 [5120, 512], P('fsdp'), may hold values from -0.078125 to 0.078125
Outputs:
- hidden_grad: bfloat16 [2048, 32, 5120], P(('dp', 'fsdp'))
- key_grad: float32 [5120, 512], P('fsdp')
- value_grad: float32 [5120, 512], P('fsdp')
Inputs may be any that keep to these rules, and one draw needn't show every extreme that they name: Within each fsdp index, every device sends 8 - 1 trajectories, one to each other dp index, and receives one from each; a slot whose send_peer is its own dp index is kept, and an arriving trajectory fills a slot whose recv_from names its sender. recv_from is the inverse of send_peer in the sense above: slot s of device (a, b) with recv_from = c != a receives the unique slot of device (c, b) whose send_peer is a.
All inputs are finite; a program needn't handle non-finite values.
Results may differ from a plain program's by a relative error of at most 0.025.
Values may be sent and summed in bfloat16 or wider, within the bound.
A program may use at most 192 MiB of HBM per device.

v0:
```python
import jax
import jax.numpy as jnp
from jax import lax
from jax.sharding import PartitionSpec as P

HD = 128
JBLK = 16


def attention_backward(hidden_rows, query_rows, grad_rows, slot_counts, key_full, value_full):
    slot_total, token_slots, width = hidden_rows.shape
    head_size = HD
    kv_heads = key_full.shape[1] // head_size
    flat_rows = hidden_rows.reshape(slot_total * token_slots, width)
    key_rows = jnp.dot(flat_rows, key_full, preferred_element_type=jnp.float32).astype(jnp.bfloat16)
    value_rows = jnp.dot(flat_rows, value_full, preferred_element_type=jnp.float32).astype(
        jnp.bfloat16
    )
    keys_split = key_rows.reshape(slot_total, token_slots, kv_heads, head_size)
    values_split = value_rows.reshape(slot_total, token_slots, kv_heads, head_size)
    query_split = query_rows.reshape(slot_total, token_slots, kv_heads, -1, head_size)
    score_scale = head_size ** (-0.5)
    scores = (
        jnp.einsum("stgrd,sugd->sgrtu", query_split, keys_split, preferred_element_type=jnp.float32)
        * score_scale
    )
    positions = jnp.arange(token_slots, dtype=jnp.float32)
    live_rows = positions[None, :] < (slot_counts * JBLK)[:, None]
    allowed = (positions[:, None] >= positions[None, :])[None, :, :] & live_rows[:, None, :]
    allowed = allowed[:, None, None, :, :]
    scores = jnp.where(allowed, scores, -1e30)
    top_score = jnp.max(scores, axis=-1, keepdims=True)
    exponent_terms = jnp.exp(scores - top_score)
    probs = exponent_terms / jnp.sum(exponent_terms, axis=-1, keepdims=True)
    probs_half = probs.astype(jnp.bfloat16)
    attended = jnp.einsum(
        "sgrtu,sugd->stgrd", probs_half, values_split, preferred_element_type=jnp.float32
    )
    row_weight = live_rows.astype(jnp.float32) / slot_counts[:, None]
    grad_split = grad_rows.reshape(slot_total, token_slots, kv_heads, -1, head_size)
    out_delta = (grad_split * row_weight[:, :, None, None, None]).astype(jnp.bfloat16)
    value_delta = jnp.einsum(
        "sgrtu,stgrd->sugd", probs_half, out_delta, preferred_element_type=jnp.float32
    ).astype(jnp.bfloat16)
    prob_delta = jnp.einsum(
        "stgrd,sugd->sgrtu", out_delta, values_split, preferred_element_type=jnp.float32
    )
    row_delta = jnp.sum(out_delta.astype(jnp.float32) * attended, axis=-1)
    row_delta = jnp.transpose(row_delta, (0, 2, 3, 1))
    score_delta = (probs * (prob_delta - row_delta[..., None]) * score_scale).astype(jnp.bfloat16)
    key_delta = jnp.einsum(
        "sgrtu,stgrd->sugd", score_delta, query_split, preferred_element_type=jnp.float32
    ).astype(jnp.bfloat16)
    key_flat = key_delta.reshape(slot_total * token_slots, -1)
    value_flat = value_delta.reshape(slot_total * token_slots, -1)
    return (flat_rows, key_flat, value_flat)


def project_back(key_flat, value_flat, key_full, value_full, out_shape):
    hidden_delta = jnp.einsum(
        "rk,dk->rd", key_flat, key_full, preferred_element_type=jnp.float32
    ) + jnp.einsum("rk,dk->rd", value_flat, value_full, preferred_element_type=jnp.float32)
    return hidden_delta.astype(jnp.bfloat16).reshape(out_shape)


def block_plan(send_peer, recv_from, own_group, group_count):
    peer_ids = jnp.arange(group_count, dtype=jnp.int32)
    staying = recv_from == own_group
    chosen = ((send_peer[None, :] == peer_ids[:, None]) & (peer_ids[:, None] != own_group)).astype(
        jnp.bfloat16
    )
    placing = (
        (recv_from[:, None] == peer_ids[None, :]) & jnp.logical_not(staying)[:, None]
    ).astype(jnp.bfloat16)
    return (chosen, placing, staying)


def select_rows(chosen, source):
    return jnp.einsum("ps,stf->ptf", chosen, source, preferred_element_type=jnp.float32).astype(
        jnp.bfloat16
    )


def settle(own_rows, incoming, placing, staying):
    arrived_rows = jnp.einsum(
        "sp,ptf->stf", placing, incoming, preferred_element_type=jnp.float32
    ).astype(jnp.bfloat16)
    return jnp.where(staying[:, None, None], own_rows, arrived_rows)


def settle_inputs(
    arrived, placing, staying, hidden, queries, out_grad, counts, key_full, value_full
):
    hidden_rows = settle(hidden, arrived[0], placing, staying)
    query_rows = settle(queries, arrived[1], placing, staying)
    grad_rows = settle(out_grad, arrived[2], placing, staying)
    moved_counts = jnp.dot(placing, arrived[3], preferred_element_type=jnp.float32)[:, 0]
    slot_counts = jnp.where(staying, counts.astype(jnp.float32), moved_counts)
    return attention_backward(hidden_rows, query_rows, grad_rows, slot_counts, key_full, value_full)


def body(hidden, queries, out_grad, counts, send_peer, recv_from, key_weight, value_weight):
    key_full, value_full = (
        lax.all_gather(key_weight, "fsdp", axis=0, tiled=True),
        lax.all_gather(value_weight, "fsdp", axis=0, tiled=True),
    )
    group_count = lax.axis_size("dp")
    own_group = lax.axis_index("dp")
    count_half = counts.astype(jnp.bfloat16)
    chosen, placing, staying = block_plan(send_peer, recv_from, own_group, group_count)
    count_out = jnp.dot(chosen, count_half[:, None], preferred_element_type=jnp.float32).astype(
        jnp.bfloat16
    )
    arrived = (
        lax.all_to_all(select_rows(chosen, hidden), "dp", split_axis=0, concat_axis=0, tiled=True),
        lax.all_to_all(select_rows(chosen, queries), "dp", split_axis=0, concat_axis=0, tiled=True),
        lax.all_to_all(
            select_rows(chosen, out_grad), "dp", split_axis=0, concat_axis=0, tiled=True
        ),
        lax.all_to_all(count_out, "dp", split_axis=0, concat_axis=0, tiled=True),
    )
    flat_rows, key_flat, value_flat = settle_inputs(
        arrived, placing, staying, hidden, queries, out_grad, counts, key_full, value_full
    )
    hidden_grad = project_back(key_flat, value_flat, key_full, value_full, hidden.shape)
    pair_delta = jnp.concatenate([key_flat, value_flat], axis=1)
    partial_rows = lax.psum_scatter(
        jnp.einsum("rd,rk->dk", flat_rows, pair_delta, preferred_element_type=jnp.float32).astype(
            jnp.bfloat16
        ),
        "fsdp",
        scatter_dimension=0,
        tiled=True,
    )
    weight_grad = lax.psum(partial_rows, "dp").astype(jnp.float32)
    key_width = key_flat.shape[1]
    return (hidden_grad, weight_grad[:, :key_width], weight_grad[:, key_width:])


def solution(mesh):
    return jax.shard_map(
        body,
        mesh=mesh,
        in_specs=(
            P(("dp", "fsdp"), None, None),
            P(("dp", "fsdp"), None, None),
            P(("dp", "fsdp"), None, None),
            P(("dp", "fsdp")),
            P(("dp", "fsdp")),
            P(("dp", "fsdp")),
            P("fsdp", None),
            P("fsdp", None),
        ),
        out_specs=(P(("dp", "fsdp"), None, None), P("fsdp", None), P("fsdp", None)),
        check_vma=False,
    )
```

profile of v0, /device:TPU:0, one launch (start us, length us, event | category | flops | bytes accessed | tf_op | source)
XLA Modules:
  0.0 400.1 jit_solution(12655756017743803781)
XLA Ops:
  10.2 6.4 %all-to-all-start.1 = ((bf16[8,1,1]{2,1,0:T(2,128)(2,1)}), bf16[8,1,1]{2,1,0:T(2,128)(2,1)S(1)}, u32[]{:S(2)}, u32[]{:S(2)}) async-start(bf16[8,1,1]{2,1,0:T(2,128)(2,1)} %copy.62), calls=%async_computation.1 | async-start | bytes 8192 | tf_op jit(solution)/shard_map/all_to_all | solution.py:120
  16.7 4.6 %convolution_convert_fusion.6 = bf16[8,32,2560]{2,0,1:T(8,128)(2,1)S(1)} fusion(bf16[16,32,2560]{2,1,0:T(8,128)(2,1)} %param.9, s32[16]{0:T(128)} %param.12, pred[8]{0:T(512)(128)(4,1)S(1)} %iota_compare_fusion.4), kind=kOutput, calls=%fused_computation.24 | convolution fusion | flops 21627136 | bytes 3932232 | tf_op jit(solution)/shard_map/ps,stf->ptf/dot_general | solution.py:79
  22.7 5.7 %all-to-all-start = ((bf16[8,32,2560]{2,1,0:T(8,128)(2,1)}), bf16[8,32,2560]{2,1,0:T(8,128)(2,1)}, u32[]{:S(2)}, u32[]{:S(2)}) async-start(bf16[8,32,2560]{2,1,0:T(8,128)(2,1)} %copy.58), calls=%async_computation | async-start | bytes 2621440 | tf_op jit(solution)/shard_map/all_to_all | solution.py:116
  32.9 13.6 %all-to-all-done = bf16[8,32,2560]{2,1,0:T(8,128)(2,1)} async-done(((bf16[8,32,2560]{2,1,0:T(8,128)(2,1)}), bf16[8,32,2560]{2,1,0:T(8,128)(2,1)}, u32[]{:S(2)}, u32[]{:S(2)}) %all-to-all-start) | async-done | bytes 1310752 | tf_op jit(solution)/shard_map/all_to_all | solution.py:116
  46.5 4.5 %all-to-all-start.3 = ((bf16[8,32,2560]{2,1,0:T(8,128)(2,1)}), bf16[8,32,2560]{2,1,0:T(8,128)(2,1)}, u32[]{:S(2)}, u32[]{:S(2)}) async-start(bf16[8,32,2560]{2,1,0:T(8,128)(2,1)} %copy.71), calls=%async_computation.3 | async-start | bytes 2621440 | tf_op jit(solution)/shard_map/all_to_all | solution.py:117
  51.0 8.1 %convolution_convert_fusion.2 = bf16[8,32,5120]{2,0,1:T(8,128)(2,1)S(1)} fusion(bf16[16,32,5120]{2,1,0:T(8,128)(2,1)} %param.8, s32[16]{0:T(128)S(1)} %copy-done.4, pred[8]{0:T(512)(128)(4,1)S(1)} %iota_compare_fusion.4), kind=kOutput, calls=%fused_computation.5 | convolution fusion | flops 43254016 | bytes 7864392 | tf_op jit(solution)/shard_map/ps,stf->ptf/dot_general | solution.py:79
  62.0 15.7 %all-to-all-done.3 = bf16[8,32,2560]{2,1,0:T(8,128)(2,1)} async-done(((bf16[8,32,2560]{2,1,0:T(8,128)(2,1)}), bf16[8,32,2560]{2,1,0:T(8,128)(2,1)}, u32[]{:S(2)}, u32[]{:S(2)}) %all-to-all-start.3) | async-done | bytes 1310752 | tf_op jit(solution)/shard_map/all_to_all | solution.py:117
  77.8 4.5 %all-to-all-start.2 = ((bf16[8,32,5120]{2,1,0:T(8,128)(2,1)}), bf16[8,32,5120]{2,1,0:T(8,128)(2,1)}, u32[]{:S(2)}, u32[]{:S(2)}) async-start(bf16[8,32,5120]{2,1,0:T(8,128)(2,1)} %copy.64), calls=%async_computation.2 | async-start | bytes 5242880 | tf_op jit(solution)/shard_map/all_to_all | solution.py:115
  82.9 7.9 %fusion.8 = bf16[16,32,2560]{2,0,1:T(8,128)(2,1)} fusion(pred[16]{0:T(512)(128)(4,1)S(1)} %get-tuple-element.4, bf16[16,32,2560]{2,1,0:T(8,128)(2,1)} %param.9, bf16[8,32,2560]{2,1,0:T(8,128)(2,1)} %all-to-all-done, s32[16]{0:T(128)S(1)} %copy-done.3, pred[16]{0:T(512)(128)(4,1)S(1)} %get-tuple-element.3), kind=kOutput, calls=%fused_computation.19 | convolution fusion | flops 23593216 | bytes 6553696 | tf_op jit(solution)/shard_map/sp,ptf->stf/dot_general | solution.py:85
  90.8 7.5 %reshape.143 = bf16[16,32,4,5,128]{4,3,2,0,1:T(8,128)(2,1)} reshape(bf16[16,32,2560]{2,0,1:T(8,128)(2,1)} %fusion.8) | data formatting | bytes 5242880 | tf_op jit(solution)/shard_map/reshape | solution.py:21
  98.4 8.0 %fusion.10 = f32[16,32,2560]{2,0,1:T(8,128)} fusion(pred[16]{0:T(512)(128)(4,1)S(1)} %get-tuple-element.4, bf16[16,32,2560]{2,1,0:T(8,128)(2,1)S(1)} %copy-done, bf16[8,32,2560]{2,1,0:T(8,128)(2,1)} %all-to-all-done.3, s32[16]{0:T(128)S(1)} %copy-done.3, pred[16]{0:T(512)(128)(4,1)S(1)} %get-tuple-element.3), kind=kOutput, calls=%fused_computation.21 | convolution fusion | flops 24903936 | bytes 9175136 | tf_op jit(solution)/shard_map/sp,ptf->stf/dot_general | solution.py:85
  106.4 8.3 %reshape.142 = f32[16,32,4,5,128]{4,3,2,0,1:T(8,128)} reshape(f32[16,32,2560]{2,0,1:T(8,128)} %fusion.10) | data formatting | bytes 10485760 | tf_op jit(solution)/shard_map/convert_element_type | solution.py:41
  114.7 8.1 %fusion.6 = bf16[16,32,4,5,128]{4,1,3,2,0:T(8,128)(2,1)S(1)} fusion(f32[16,32,4,5,128]{4,3,2,0,1:T(8,128)} %reshape.142, f32[16,32]{1,0:T(8,128)S(1)} %convert_divide_fusion), kind=kLoop, calls=%fused_computation.13 | loop fusion | flops 2621440 | bytes 7866368 | tf_op jit(solution)/shard_map/convert_element_type | solution.py:41
  122.8 13.3 %fusion.1 = bf16[16,32,5120]{2,0,1:T(8,128)(2,1)S(1)} fusion(pred[16]{0:T(512)(128)(4,1)S(1)} %get-tuple-element.4, bf16[16,32,5120]{2,1,0:T(8,128)(2,1)} %param.8, bf16[8,32,5120]{2,1,0:T(8,128)(2,1)} %all-to-all-done.2, s32[16]{0:T(128)S(1)} %copy-done.3, pred[16]{0:T(512)(128)(4,1)S(1)} %get-tuple-element.3), kind=kOutput, calls=%fused_computation.4 | convolution fusion | flops 47186176 | bytes 13107296 | tf_op jit(solution)/shard_map/sp,ptf->stf/dot_general | solution.py:85
  136.1 5.2 %copy.67 = bf16[16,32,5120]{2,1,0:T(8,128)(2,1)} copy(bf16[16,32,5120]{2,0,1:T(8,128)(2,1)S(1)} %fusion.1) | data formatting | bytes 10485760 | tf_op jit(solution)/shard_map/jit(_where)/select_n | solution.py:88
  141.3 7.2 %convolution_convert_fusion.8 = bf16[512,512]{1,0:T(8,128)(2,1)S(1)} fusion(bf16[512,5120]{1,0:T(8,128)(2,1)} %bitcast.109, bf16[5120,512]{1,0:T(8,128)(2,1)} %all-gather.3.cloned.1.call-done), kind=kOutput, calls=%fused_computation.46 | convolution fusion | flops 2684616704 | bytes 11010048 | tf_op jit(solution)/shard_map/dot_general | solution.py:15
  149.4 7.7 %convolution_convert_fusion.7 = bf16[512,512]{1,0:T(8,128)(2,1)} fusion(bf16[512,5120]{1,0:T(8,128)(2,1)} %bitcast.110, bf16[5120,512]{1,0:T(8,128)(2,1)} %all-gather.5.cloned.1.call-done), kind=kOutput, calls=%fused_computation.45 | convolution fusion | flops 2684616704 | bytes 11010048 | tf_op jit(solution)/shard_map/dot_general | solution.py:16
  158.3 6.0 %fusion.25 = f32[16,4,32,32,5]{3,2,4,1,0:T(8,128)S(1)} fusion(bf16[16,32,4,5,128]{4,3,2,0,1:T(8,128)(2,1)} %reshape.143, bf16[16,32,4,128,1]{3,2,1,0,4:T(4,128)(2,1)} %bitcast.117), kind=kOutput, calls=%fused_computation.37 | convolution fusion | flops 83886080 | bytes 4456448 | tf_op jit(solution)/shard_map/stgrd,sugd->sgrtu/dot_general | solution.py:24
  175.6 10.3 %fusion.42 = bf16[16,32,4,128]{3,1,2,0:T(8,128)(2,1)} fusion(bf16[16,32,4,5,128]{4,3,2,0,1:T(8,128)(2,1)} %reshape.143, bf16[16,32,4,5,128]{4,1,3,2,0:T(8,128)(2,1)S(1)} %fusion.6, f32[16,4,5,32]{3,2,1,0:T(8,128)S(1)} %copy.80, f32[16,4,5,32,32]{3,4,2,1,0:T(8,128)} %copy-done.1, f32[16,4,5,32]{3,2,1,0:T(8,128)} %copy-done.2, ...), kind=kOutput, calls=%fused_computation.49 | convolution fusion | flops 169672704 | bytes 7684096 | tf_op jit(solution)/shard_map/sgrtu,stgrd->sugd/dot_general | solution.py:51
  188.7 10.8 %convolution_convert_fusion = bf16[5120,1024]{1,0:T(8,128)(2,1)} fusion(bf16[512,5120]{1,0:T(8,128)(2,1)} %bitcast.111, bf16[512,512]{1,0:T(8,128)(2,1)S(1)} %get-tuple-element.11, bf16[512,512]{1,0:T(8,128)(2,1)S(1)} %get-tuple-element.12), kind=kOutput, calls=%fused_computation.2 | convolution fusion | flops 5376049152 | bytes 16777216 | tf_op jit(solution)/shard_map/rd,rk->dk/dot_general | solution.py:128
  199.6 8.3 %fusion.90 = f32[512,5120]{1,0:T(8,128)} fusion(bf16[5120,512]{1,0:T(8,128)(2,1)} %all-gather.3.cloned.1.call-done, bf16[64,8,4,128]{3,2,1,0:T(4,128)(2,1)S(1)} %bitcast.113), kind=kOutput, calls=%fused_computation.98 | convolution fusion | flops 2684354560 | bytes 16252928 | tf_op jit(solution)/shard_map/rk,dk->rd/dot_general | solution.py:60
  207.9 104.8 %reduce-scatter.2.cloned.1.call-done = bf16[320,1024]{1,0:T(8,128)(2,1)} async-done(((bf16[5120,1024]{1,0:T(8,128)(2,1)}), bf16[320,1024]{1,0:T(8,128)(2,1)}) %reduce-scatter.2.cloned.1.call-update) | async-done | bytes 655376 | tf_op jit(solution)/shard_map/reduce_scatter | solution.py:127
  312.7 8.7 %add_convert_fusion = bf16[512,5120]{1,0:T(8,128)(2,1)} fusion(f32[512,5120]{1,0:T(8,128)} %fusion.90, bf16[5120,512]{1,0:T(8,128)(2,1)} %all-gather.5.cloned.1.call-done, bf16[64,8,4,128]{3,2,1,0:T(4,128)(2,1)S(1)} %bitcast.119), kind=kOutput, calls=%fused_computation.1 | convolution fusion | flops 2689597440 | bytes 21495808 | tf_op jit(solution)/shard_map/rk,dk->rd/dot_general | solution.py:62
  321.4 69.5 %all-reduce.2.cloned.1.call-done = bf16[320,1024]{1,0:T(8,128)(2,1)} async-done(((bf16[320,1024]{1,0:T(8,128)(2,1)}), bf16[320,1024]{1,0:T(8,128)(2,1)}) %all-reduce.2.cloned.1.call-update) | async-done | bytes 655376 | tf_op jit(solution)/shard_map/psum | solution.py:135
  (50 shorter events, 30.8 us)
Async XLA Ops:
  7.2 21.3 %copy-start.4 = (s32[16]{0:T(128)S(1)}, s32[16]{0:T(128)}, u32[]{:S(2)}) copy-start(s32[16]{0:T(128)} %param.12) | copy-start | bytes 196
  7.2 21.3 %copy-start = (bf16[16,32,2560]{2,1,0:T(8,128)(2,1)S(1)}, bf16[16,32,2560]{2,1,0:T(8,128)(2,1)}, u32[]{:S(2)}) copy-start(bf16[16,32,2560]{2,1,0:T(8,128)(2,1)} %param.10) | copy-start | bytes 7864324
  7.2 134.1 %all-gather.3.cloned.1.call-start = ((), (), s32[]{:S(2)}) async-start(), calls=%async_computation.5 | async-start | bytes 5570560 | tf_op jit(solution)/shard_map/all_gather | solution.py:104
  7.9 141.5 %all-gather.5.cloned.1.call-start = ((), (), s32[]{:S(2)}) async-start(), calls=%async_computation.6 | async-start | bytes 5570560 | tf_op jit(solution)/shard_map/all_gather | solution.py:105
  10.2 12.5 %all-to-all-start.1 = ((bf16[8,1,1]{2,1,0:T(2,128)(2,1)}), bf16[8,1,1]{2,1,0:T(2,128)(2,1)S(1)}, u32[]{:S(2)}, u32[]{:S(2)}) async-start(bf16[8,1,1]{2,1,0:T(2,128)(2,1)} %copy.62), calls=%async_computation.1 | async-start | bytes 8192 | tf_op jit(solution)/shard_map/all_to_all | solution.py:120
  22.7 23.8 %all-to-all-start = ((bf16[8,32,2560]{2,1,0:T(8,128)(2,1)}), bf16[8,32,2560]{2,1,0:T(8,128)(2,1)}, u32[]{:S(2)}, u32[]{:S(2)}) async-start(bf16[8,32,2560]{2,1,0:T(8,128)(2,1)} %copy.58), calls=%async_computation | async-start | bytes 2621440 | tf_op jit(solution)/shard_map/all_to_all | solution.py:116
  46.5 31.3 %all-to-all-start.3 = ((bf16[8,32,2560]{2,1,0:T(8,128)(2,1)}), bf16[8,32,2560]{2,1,0:T(8,128)(2,1)}, u32[]{:S(2)}, u32[]{:S(2)}) async-start(bf16[8,32,2560]{2,1,0:T(8,128)(2,1)} %copy.71), calls=%async_computation.3 | async-start | bytes 2621440 | tf_op jit(solution)/shard_map/all_to_all | solution.py:117
  59.1 23.2 %copy-start.3 = (s32[16]{0:T(128)S(1)}, s32[16]{0:T(128)}, u32[]{:S(2)}) copy-start(s32[16]{0:T(128)} %param.13) | copy-start | bytes 196
  59.1 23.4 %copy-start.5 = (s32[16]{0:T(128)S(1)}, s32[16]{0:T(128)}, u32[]{:S(2)}) copy-start(s32[16]{0:T(128)} %param.11) | copy-start | bytes 196
  77.8 45.0 %all-to-all-start.2 = ((bf16[8,32,5120]{2,1,0:T(8,128)(2,1)}), bf16[8,32,5120]{2,1,0:T(8,128)(2,1)}, u32[]{:S(2)}, u32[]{:S(2)}) async-start(bf16[8,32,5120]{2,1,0:T(8,128)(2,1)} %copy.64), calls=%async_computation.2 | async-start | bytes 5242880 | tf_op jit(solution)/shard_map/all_to_all | solution.py:115
  82.3 230.4 %reduce-scatter.2.cloned.1.call-start = ((), (), s32[]{:S(2)}) async-start(), calls=%async_computation.7 | async-start | bytes 11141120 | tf_op jit(solution)/shard_map/reduce_scatter | solution.py:127
  166.7 3.1 copy-start.1
  166.7 3.1 copy-start.2
  199.5 191.4 %all-reduce.2.cloned.1.call-start = ((), (), s32[]{:S(2)}) async-start(), calls=%async_computation.8 | async-start | bytes 1310720 | tf_op jit(solution)/shard_map/psum | solution.py:135
Sparse Core Ops, SparseCore 0:
  10.4 71.5 all-gather.2
  84.5 60.8 all-gather.4
  199.6 112.9 reduce-scatter.1
  315.1 75.6 all-reduce.1
where the time goes:
time: 407 us; the launch traced here: 400 us
  waiting for transfers between devices  205 us (50%)
  matrix products  110 us (27%)
  local copies, waits for them, and re-layouts  37.9 us (9%)
  starting transfers between devices  21.2 us (5%)
  between operations  14.4 us (4%)
  other arithmetic  11.8 us (3%)
    reduce_scatter x1, waiting for transfers between devices, body(): lax.psum_scatter(jnp.einsum('rd,rk->dk', flat_rows, pair_delta, preferred...  105 us
    psum x1, waiting for transfers between devices, body(): weight_grad = lax.psum(partial_rows, 'dp').astype(jnp.float32)  69.5 us
    dot_general x3, matrix products, settle(): jnp.einsum('sp,ptf->stf', placing, incoming, preferred_element_type=jnp.f...  29.2 us
    all_to_all x1, waiting for transfers between devices, body(): lax.all_to_all(select_rows(chosen, out_grad), 'dp', split_axis=0, concat_...  15.7 us
    dot_general x3, matrix products, select_rows(): jnp.einsum('ps,stf->ptf', chosen, source, preferred_element_type=jnp.floa...  15.7 us
    all_to_all x1, waiting for transfers between devices, body(): lax.all_to_all(select_rows(chosen, queries), 'dp', split_axis=0, concat_a...  13.6 us
    dot_general x1, matrix products, body(): jnp.einsum('rd,rk->dk', flat_rows, pair_delta, preferred_element_type=jnp...  10.8 us
    dot_general x1, matrix products, attention_backward(): jnp.einsum('sgrtu,stgrd->sugd', score_delta, query_split, preferred_eleme...  10.3 us
  transfers between devices with their start and end apart: 8, of which 4 were waited for; matrix products, arithmetic and copies ran while one was open for 27% of the time, Pallas kernels for 0%

commit v1 on v0

--- a/solution.py
+++ b/solution.py
@@ -56,13 +56,6 @@
     return (flat_rows, key_flat, value_flat)
 
 
-def project_back(key_flat, value_flat, key_full, value_full, out_shape):
-    hidden_delta = jnp.einsum(
-        "rk,dk->rd", key_flat, key_full, preferred_element_type=jnp.float32
-    ) + jnp.einsum("rk,dk->rd", value_flat, value_full, preferred_element_type=jnp.float32)
-    return hidden_delta.astype(jnp.bfloat16).reshape(out_shape)
-
-
 def block_plan(send_peer, recv_from, own_group, group_count):
     peer_ids = jnp.arange(group_count, dtype=jnp.int32)
     staying = recv_from == own_group
@@ -88,42 +81,24 @@
     return jnp.where(staying[:, None, None], own_rows, arrived_rows)
 
 
-def settle_inputs(
-    arrived, placing, staying, hidden, queries, out_grad, counts, key_full, value_full
-):
-    hidden_rows = settle(hidden, arrived[0], placing, staying)
-    query_rows = settle(queries, arrived[1], placing, staying)
-    grad_rows = settle(out_grad, arrived[2], placing, staying)
-    moved_counts = jnp.dot(placing, arrived[3], preferred_element_type=jnp.float32)[:, 0]
-    slot_counts = jnp.where(staying, counts.astype(jnp.float32), moved_counts)
-    return attention_backward(hidden_rows, query_rows, grad_rows, slot_counts, key_full, value_full)
-
-
 def body(hidden, queries, out_grad, counts, send_peer, recv_from, key_weight, value_weight):
-    key_full, value_full = (
-        lax.all_gather(key_weight, "fsdp", axis=0, tiled=True),
-        lax.all_gather(value_weight, "fsdp", axis=0, tiled=True),
+    width = key_weight.shape[1]
+    pair_full = lax.all_gather(
+        jnp.concatenate([key_weight, value_weight], axis=1), "fsdp", axis=0, tiled=True
     )
+    key_full, value_full = pair_full[:, :width], pair_full[:, width:]
     group_count = lax.axis_size("dp")
     own_group = lax.axis_index("dp")
-    count_half = counts.astype(jnp.bfloat16)
     chosen, placing, staying = block_plan(send_peer, recv_from, own_group, group_count)
-    count_out = jnp.dot(chosen, count_half[:, None], preferred_element_type=jnp.float32).astype(
-        jnp.bfloat16
+    flat_rows, key_flat, value_flat = attention_backward(
+        hidden, queries, out_grad, counts.astype(jnp.float32), key_full, value_full
     )
-    arrived = (
-        lax.all_to_all(select_rows(chosen, hidden), "dp", split_axis=0, concat_axis=0, tiled=True),
-        lax.all_to_all(select_rows(chosen, queries), "dp", split_axis=0, concat_axis=0, tiled=True),
-        lax.all_to_all(
-            select_rows(chosen, out_grad), "dp", split_axis=0, concat_axis=0, tiled=True
-        ),
-        lax.all_to_all(count_out, "dp", split_axis=0, concat_axis=0, tiled=True),
+    pair_delta = jnp.concatenate([key_flat, value_flat], axis=1)
+    slots, tokens = hidden.shape[0], hidden.shape[1]
+    pair_rows = pair_delta.reshape(slots, tokens, 2 * width)
+    arrived = lax.all_to_all(
+        select_rows(chosen, pair_rows), "dp", split_axis=0, concat_axis=0, tiled=True
     )
-    flat_rows, key_flat, value_flat = settle_inputs(
-        arrived, placing, staying, hidden, queries, out_grad, counts, key_full, value_full
-    )
-    hidden_grad = project_back(key_flat, value_flat, key_full, value_full, hidden.shape)
-    pair_delta = jnp.concatenate([key_flat, value_flat], axis=1)
     partial_rows = lax.psum_scatter(
         jnp.einsum("rd,rk->dk", flat_rows, pair_delta, preferred_element_type=jnp.float32).astype(
             jnp.bfloat16
@@ -132,9 +107,14 @@
         scatter_dimension=0,
         tiled=True,
     )
+    settled = settle(pair_rows, arrived, placing, staying).reshape(slots * tokens, 2 * width)
+    hidden_grad = (
+        jnp.einsum("rk,dk->rd", settled, pair_full, preferred_element_type=jnp.float32)
+        .astype(jnp.bfloat16)
+        .reshape(hidden.shape)
+    )
     weight_grad = lax.psum(partial_rows, "dp").astype(jnp.float32)
-    key_width = key_flat.shape[1]
-    return (hidden_grad, weight_grad[:, :key_width], weight_grad[:, key_width:])
+    return (hidden_grad, weight_grad[:, :width], weight_grad[:, width:])
 
 
 def solution(mesh):

time: 407 us -> 370 us (0.909)
  the two profiles are of different devices: /device:TPU:0 before, /device:TPU:1 now
where the time goes in v1:
time: 370 us; the launch traced here: 365 us
  waiting for transfers between devices  229 us (62%)
  matrix products  57.4 us (16%)
  local copies, waits for them, and re-layouts  46.7 us (13%)
  other arithmetic  14.2 us (4%)
  between operations  14 us (4%)
  starting transfers between devices  4.3 us (1%)
    unnamed x4, waiting for transfers between devices  90.7 us
    all_gather x1, waiting for transfers between devices, body(): lax.all_gather(jnp.concatenate([key_weight, value_weight], axis=1), 'fsdp...  66 us
    psum x1, waiting for transfers between devices, body(): weight_grad = lax.psum(partial_rows, 'dp').astype(jnp.float32)  62.6 us
    unnamed x22, local copies, waits for them, and re-layouts  21.4 us
    dot_general x1, matrix products, body(): jnp.einsum('rk,dk->rd', settled, pair_full, preferred_element_type=jnp.fl...  11.3 us
    dot_general x1, matrix products, body(): jnp.einsum('rd,rk->dk', flat_rows, pair_delta, preferred_element_type=jnp...  11 us
    dot_general x1, matrix products, attention_backward(): jnp.einsum('sgrtu,stgrd->sugd', score_delta, query_split, preferred_eleme...  9.74 us
    all_to_all x1, waiting for transfers between devices, body(): lax.all_to_all(select_rows(chosen, pair_rows), 'dp', split_axis=0, concat...  9.29 us
  transfers between devices with their start and end apart: 4, of which 4 were waited for; matrix products, arithmetic and copies ran while one was open for 10% of the time, Pallas kernels for 0%

profile of v1, /device:TPU:1, one launch (start us, length us, event | category | flops | bytes accessed | tf_op | source)
XLA Modules:
  0.0 365.2 jit_solution(45866226247940863)
XLA Ops:
  7.2 2.1 pad_maximum_fusion
  9.4 7.1 %reshape.118 = bf16[16,32,4,5,128]{4,3,2,1,0:T(8,128)(2,1)} reshape(bf16[16,32,2560]{2,1,0:T(8,128)(2,1)} %param.9) | data formatting | bytes 5242880 | tf_op jit(solution)/shard_map/reshape | solution.py:21
  16.5 4.8 %reshape.124 = f32[16,32,4,5,128]{4,3,2,1,0:T(8,128)} reshape(bf16[16,32,2560]{2,1,0:T(8,128)(2,1)S(1)} %copy-done.1) | data formatting | bytes 7864320 | tf_op jit(solution)/shard_map/convert_element_type | solution.py:41
  21.6 8.5 %fusion.9 = bf16[16,32,4,5,128]{4,1,3,2,0:T(8,128)(2,1)S(1)} fusion(f32[16,32,4,5,128]{4,3,2,1,0:T(8,128)} %reshape.124, f32[16,32]{1,0:T(8,128)S(1)} %convert_divide_fusion), kind=kLoop, calls=%fused_computation.15 | loop fusion | flops 2621440 | bytes 7866368 | tf_op jit(solution)/shard_map/convert_element_type | solution.py:41
  30.1 66.0 %all-gather.2.cloned.1.call-done = bf16[5120,1024]{1,0:T(8,128)(2,1)} async-done(((bf16[320,1024]{1,0:T(8,128)(2,1)}), bf16[5120,1024]{1,0:T(8,128)(2,1)}) %all-gather.2.cloned.1.call-update) | async-done | bytes 10485776 | tf_op jit(solution)/shard_map/all_gather | solution.py:86
  96.1 7.0 %fusion.45 = bf16[512,512]{0,1:T(8,128)(2,1)S(1)} fusion(bf16[512,5120]{1,0:T(8,128)(2,1)} %bitcast.97, bf16[5120,1024]{1,0:T(8,128)(2,1)} %all-gather.2.cloned.1.call-done), kind=kOutput, calls=%fused_computation.40 | convolution fusion | flops 2684616704 | bytes 11010048 | tf_op jit(solution)/shard_map/dot_general | solution.py:15
  105.3 7.8 %fusion.42 = bf16[512,512]{0,1:T(8,128)(2,1)} fusion(bf16[512,5120]{1,0:T(8,128)(2,1)} %bitcast.98, bf16[5120,1024]{1,0:T(8,128)(2,1)} %all-gather.2.cloned.1.call-done), kind=kOutput, calls=%fused_computation.39 | convolution fusion | flops 2684616704 | bytes 11010048 | tf_op jit(solution)/shard_map/dot_general | solution.py:16
  113.0 2.0 copy.35
  115.1 2.0 reshape.119
  117.0 6.0 %fusion.22 = f32[16,4,32,32,5]{3,2,4,1,0:T(8,128)S(1)} fusion(bf16[16,32,4,5,128]{4,3,2,1,0:T(8,128)(2,1)} %reshape.118, bf16[16,32,4,128,1]{3,2,1,0,4:T(4,128)(2,1)S(1)} %bitcast.93), kind=kOutput, calls=%fused_computation.28 | convolution fusion | flops 83886080 | bytes 4456448 | tf_op jit(solution)/shard_map/stgrd,sugd->sgrtu/dot_general | solution.py:24
  123.1 2.3 fusion.78
  126.4 1.4 fusion.48
  127.8 2.4 fusion.5
  130.2 1.4 copy.72
  131.6 1.7 copy.41
  133.3 9.7 %fusion.49 = bf16[16,32,4,128]{3,1,2,0:T(8,128)(2,1)} fusion(bf16[16,32,4,5,128]{4,3,2,1,0:T(8,128)(2,1)} %reshape.118, bf16[16,32,4,5,128]{4,1,3,2,0:T(8,128)(2,1)S(1)} %fusion.9, f32[16,4,5,32]{3,2,1,0:T(8,128)S(1)} %copy.41, f32[16,4,5,32,32]{3,4,2,1,0:T(8,128)} %copy-done, f32[16,4,5,32]{3,2,1,0:T(8,128)} %copy-done.4, ...), kind=kOutput, calls=%fused_computation.42 | convolution fusion | flops 169672704 | bytes 7684096 | tf_op jit(solution)/shard_map/sgrtu,stgrd->sugd/dot_general | solution.py:51
  144.8 11.0 %convert_bitcast_fusion = bf16[5120,1024]{0,1:T(8,128)(2,1)} fusion(bf16[512,5120]{1,0:T(8,128)(2,1)} %bitcast.99, bf16[512,512]{1,0:T(8,128)(2,1)S(1)} %get-tuple-element.18, bf16[512,512]{1,0:T(8,128)(2,1)S(1)} %get-tuple-element.19), kind=kOutput, calls=%fused_computation.1 | convolution fusion | flops 5376049152 | bytes 16777216 | tf_op jit(solution)/shard_map/rd,rk->dk/dot_general | solution.py:103
  155.8 14.4 %copy.68 = bf16[5120,1024]{1,0:T(8,128)(2,1)} copy(bf16[5120,1024]{0,1:T(8,128)(2,1)} %convert_bitcast_fusion) | data formatting | bytes 20971520
  173.8 4.2 %all-to-all-start = ((bf16[8,32,1024]{2,1,0:T(8,128)(2,1)}), bf16[8,32,1024]{2,1,0:T(8,128)(2,1)S(1)}, u32[]{:S(2)}, u32[]{:S(2)}) async-start(bf16[8,32,1024]{2,1,0:T(8,128)(2,1)} %copy.47), calls=%async_computation | async-start | bytes 1048576 | tf_op jit(solution)/shard_map/all_to_all | solution.py:99
  178.1 9.3 %all-to-all-done = bf16[8,32,1024]{2,1,0:T(8,128)(2,1)S(1)} async-done(((bf16[8,32,1024]{2,1,0:T(8,128)(2,1)}), bf16[8,32,1024]{2,1,0:T(8,128)(2,1)S(1)}, u32[]{:S(2)}, u32[]{:S(2)}) %all-to-all-start) | async-done | bytes 524320 | tf_op jit(solution)/shard_map/all_to_all | solution.py:99
  188.5 90.7 %reduce-scatter.4.cloned.1.call-done = bf16[320,1024]{1,0:T(8,128)(2,1)} async-done(((bf16[5120,1024]{1,0:T(8,128)(2,1)}), bf16[320,1024]{1,0:T(8,128)(2,1)}) %reduce-scatter.4.cloned.1.call-update) | async-done | bytes 655376
  279.1 2.2 copy.69
  281.4 11.3 %convolution_convert_fusion = bf16[512,5120]{1,0:T(8,128)(2,1)} fusion(bf16[512,1024]{1,0:T(8,128)(2,1)S(1)} %bitcast.96, bf16[5120,1024]{1,0:T(8,128)(2,1)} %all-gather.2.cloned.1.call-done), kind=kOutput, calls=%fused_computation.2 | convolution fusion | flops 5371330560 | bytes 16777216 | tf_op jit(solution)/shard_map/rk,dk->rd/dot_general | solution.py:112
  292.7 62.6 %all-reduce.2.cloned.1.call-done = bf16[320,1024]{0,1:T(8,128)(2,1)} async-done(((bf16[320,1024]{0,1:T(8,128)(2,1)}), bf16[320,1024]{0,1:T(8,128)(2,1)}) %all-reduce.2.cloned.1.call-update) | async-done | bytes 655376 | tf_op jit(solution)/shard_map/psum | solution.py:116
  (49 shorter events, 13.4 us)
Async XLA Ops:
  7.2 9.3 %copy-start.1 = (bf16[16,32,2560]{2,1,0:T(8,128)(2,1)S(1)}, bf16[16,32,2560]{2,1,0:T(8,128)(2,1)}, u32[]{:S(2)}) copy-start(bf16[16,32,2560]{2,1,0:T(8,128)(2,1)} %param.10) | copy-start | bytes 7864324
  7.2 88.9 %all-gather.2.cloned.1.call-start = ((), (), s32[]{:S(2)}) async-start(), calls=%async_computation.2 | async-start | bytes 11141120 | tf_op jit(solution)/shard_map/all_gather | solution.py:86
  9.4 269.7 %reduce-scatter.4.cloned.1.call-start = ((), (), s32[]{:S(2)}) async-start(), calls=%async_computation.4 | async-start | bytes 11141120
  16.5 4.8 %copy-start.7 = (s32[16]{0:T(128)S(1)}, s32[16]{0:T(128)}, u32[]{:S(2)}) copy-start(s32[16]{0:T(128)} %param.11) | copy-start | bytes 196
  125.4 2.4 copy-start
  125.4 2.4 copy-start.4
  125.4 2.4 copy-start.2
  170.2 1.0 copy-start.3
  170.2 2.1 copy-start.6
  170.2 7.8 %copy-start.5 = (s32[16]{0:T(128)S(1)}, s32[16]{0:T(128)}, u32[]{:S(2)}) copy-start(s32[16]{0:T(128)} %param.13) | copy-start | bytes 196
  173.8 13.5 %all-to-all-start = ((bf16[8,32,1024]{2,1,0:T(8,128)(2,1)}), bf16[8,32,1024]{2,1,0:T(8,128)(2,1)S(1)}, u32[]{:S(2)}, u32[]{:S(2)}) async-start(bf16[8,32,1024]{2,1,0:T(8,128)(2,1)} %copy.47), calls=%async_computation | async-start | bytes 1048576 | tf_op jit(solution)/shard_map/all_to_all | solution.py:99
  178.0 177.3 %all-reduce.2.cloned.1.call-start = ((), (), s32[]{:S(2)}) async-start(), calls=%async_computation.3 | async-start | bytes 1572864 | tf_op jit(solution)/shard_map/psum | solution.py:116
Sparse Core Ops, SparseCore 0:
  11.0 85.0 all-gather.1
  170.3 108.7 reduce-scatter.3
  281.8 73.4 all-reduce.1

commit v2 on v1

--- a/solution.py
+++ b/solution.py
@@ -1,21 +1,224 @@
 import jax
 import jax.numpy as jnp
 from jax import lax
+from jax.experimental import pallas as pl
+from jax.experimental.pallas import tpu as pltpu
 from jax.sharding import PartitionSpec as P
 
 HD = 128
 JBLK = 16
-
-
-def attention_backward(hidden_rows, query_rows, grad_rows, slot_counts, key_full, value_full):
+WIDE = 384
+MESH = pl.DeviceIdType.MESH
+
+
+def place():
+    d, f = lax.axis_index("dp"), lax.axis_index("fsdp")
+    return lax.rem(lax.div(f, 2), 4), lax.div(f, 8), lax.rem(d, 2), lax.div(d, 2), lax.rem(f, 2)
+
+
+def device(x, h, l, z, c):
+    return (z * 2 + l, (h * 4 + x) * 2 + c)
+
+
+def gather_kernel(hidden, kw, vw, pair_out, w_out, w, hid, send_sem, recv_sem, local_sem):
+    x, h, l, z, c = place()
+    rows, width = kw.shape
+    cols = 2 * width
+    quarter = rows // 4
+
+    def wrap(v):
+        return lax.rem(v + 4, 4)
+
+    xp, xm = device(wrap(x + 1), h, l, z, c), device(wrap(x - 1), h, l, z, c)
+    zp, zm = device(x, h, l, wrap(z + 1), c), device(x, h, l, wrap(z - 1), c)
+    yo, peer = device(x, 1 - h, 1 - l, z, c), device(x, h, l, z, 1 - c)
+
+    hid_copy = pltpu.make_async_copy(hidden, hid, local_sem.at[0])
+    hid_copy.start()
+    own = (h * 4 + x) * 2 + c
+    w[own, :, pl.ds(0, width)] = kw[...]
+    w[own, :, pl.ds(width, width)] = vw[...]
+
+    barrier = pltpu.get_barrier_semaphore()
+    for other in (xp, xm, zp, zm, yo, peer):
+        pl.semaphore_signal(barrier, inc=1, device_id=other, device_id_type=MESH)
+    pl.semaphore_wait(barrier, 6)
+
+    number = {}
+    started = []
+
+    def copy(name, f, row, col, target):
+        i = number.setdefault(name, len(number))
+        ref = w.at[f, pl.ds(*row), pl.ds(*col)]
+        return pltpu.make_async_remote_copy(
+            src_ref=ref, dst_ref=ref, send_sem=send_sem.at[i], recv_sem=recv_sem.at[i],
+            device_id=target, device_id_type=MESH,
+        )
+
+    def send(name, f, row, col, target):
+        one = copy(name, f, row, col, target)
+        one.start()
+        started.append(one)
+
+    def arrive(name, f, row, col):
+        copy(name, f, row, col, peer).wait_recv()
+
+    def block(hh, dx, core=c):
+        return (hh * 4 + wrap(x + dx)) * 2 + core
+
+    def part(dz):
+        return (pl.multiple_of(wrap(z + dz) * quarter, quarter), quarter)
+
+    def halves(odd):
+        first = 256 if odd else 384
+        return (WIDE, first), (WIDE + first, cols - WIDE - first)
+
+    side = (h, 1 - h)
+    narrow, wide = (WIDE, cols - WIDE), (0, WIDE)
+    whole, low, high = (0, rows), (0, rows // 2), (rows // 2, rows // 2)
+
+    send("cy", own, part(0), narrow, yo)
+    send("cxp0", own, part(0), narrow, xp)
+    send("cxm0", own, part(0), narrow, xm)
+    send("own", own, whole, (0, cols), peer)
+
+    def along_z(b, f):
+        send(f"zp{b}", f, part(0), narrow, zp)
+        send(f"zm{b}", f, part(0), narrow, zm)
+
+    order = [(1, 0), (0, -1), (0, 1), (1, -1), (1, 1), (0, 2), (1, 2)]
+    arrive("cy", block(side[1], 0), part(0), narrow)
+    send("cxp1", block(side[1], 0), part(0), narrow, xp)
+    send("cxm1", block(side[1], 0), part(0), narrow, xm)
+    along_z(0, block(side[1], 0))
+    for s in (0, 1):
+        one, two = halves(s)
+        arrive(f"cxp{s}", block(side[s], -1), part(0), narrow)
+        send(f"cfp{s}", block(side[s], -1), part(0), one, xp)
+        along_z(1 + 2 * s, block(side[s], -1))
+        arrive(f"cxm{s}", block(side[s], 1), part(0), narrow)
+        send(f"cfm{s}", block(side[s], 1), part(0), two, xm)
+        along_z(2 + 2 * s, block(side[s], 1))
+    send("ay", own, whole, wide, yo)
+    send("axp0", own, whole, wide, xp)
+    send("axm0", own, whole, wide, xm)
+    for s in (0, 1):
+        one, two = halves(s)
+        arrive(f"cfp{s}", block(side[s], 2), part(0), one)
+        arrive(f"cfm{s}", block(side[s], 2), part(0), two)
+        along_z(5 + s, block(side[s], 2))
+
+    def forward_z(b):
+        s, dx = order[b]
+        one, two = halves(b % 2)
+        f = block(side[s], dx)
+        arrive(f"zp{b}", f, part(-1), narrow)
+        send(f"zfp{b}", f, part(-1), one, zp)
+        arrive(f"zm{b}", f, part(1), narrow)
+        send(f"zfm{b}", f, part(1), two, zm)
+
+    def finish_z(b):
+        s, dx = order[b]
+        one, two = halves(b % 2)
+        f = block(side[s], dx)
+        arrive(f"zfp{b}", f, part(2), one)
+        arrive(f"zfm{b}", f, part(2), two)
+        send(f"pc{b}", f, whole, narrow, peer)
+
+    def forward_x(s):
+        arrive(f"axp{s}", block(side[s], -1), whole, wide)
+        send(f"afp{s}", block(side[s], -1), low, wide, xp)
+        arrive(f"axm{s}", block(side[s], 1), whole, wide)
+        send(f"afm{s}", block(side[s], 1), high, wide, xm)
+        send(f"pa{1 + 2 * s}", block(side[s], -1), whole, wide, peer)
+        send(f"pa{2 + 2 * s}", block(side[s], 1), whole, wide, peer)
+
+    forward_z(0)
+    forward_z(1)
+    arrive("ay", block(side[1], 0), whole, wide)
+    send("axp1", block(side[1], 0), whole, wide, xp)
+    send("axm1", block(side[1], 0), whole, wide, xm)
+    send("pa0", block(side[1], 0), whole, wide, peer)
+    forward_z(2)
+    forward_z(3)
+    forward_x(0)
+    forward_z(4)
+    forward_z(5)
+    finish_z(0)
+    finish_z(1)
+    forward_z(6)
+    forward_x(1)
+    for b in range(2, 6):
+        finish_z(b)
+    for s in (0, 1):
+        arrive(f"afp{s}", block(side[s], 2), low, wide)
+        arrive(f"afm{s}", block(side[s], 2), high, wide)
+        send(f"pa{5 + s}", block(side[s], 2), whole, wide, peer)
+    finish_z(6)
+    arrive("own", block(side[0], 0, 1 - c), whole, (0, cols))
+    for b in range(7):
+        s, dx = order[b]
+        arrive(f"pa{b}", block(side[s], dx, 1 - c), whole, wide)
+        arrive(f"pc{b}", block(side[s], dx, 1 - c), whole, narrow)
+    w_copy = pltpu.make_async_copy(w, w_out, local_sem.at[1])
+    w_copy.start()
+    hid_copy.wait()
+
+    blocks = w.shape[0]
+    tokens = hidden.shape[0] * hidden.shape[1]
+    group = 4
+
+    @pl.loop(0, cols // 256)
+    def _(n):
+        at = pl.ds(pl.multiple_of(n * 256, 256), 256)
+        total = jnp.zeros((tokens, 256), jnp.float32)
+        for k in range(blocks // group):
+            left = hid[:, :, pl.ds(k * group * rows, group * rows)].reshape(tokens, group * rows)
+            right = w[pl.ds(k * group, group), :, at].reshape(group * rows, 256)
+            total = total + jnp.dot(left, right, preferred_element_type=jnp.float32)
+        pair_out[:, at] = total.astype(jnp.bfloat16)
+
+    w_copy.wait()
+    for one in started:
+        one.wait_send()
+
+
+def gather_project(hidden, key_weight, value_weight):
+    rows, width = key_weight.shape
+    tokens = hidden.shape[0] * hidden.shape[1]
+    blocks = lax.axis_size("fsdp")
+    vmem = pl.BlockSpec(memory_space=pltpu.VMEM)
+    hbm = pl.BlockSpec(memory_space=pl.ANY)
+    return pl.pallas_call(
+        gather_kernel,
+        name="gather_project",
+        out_shape=(
+            jax.ShapeDtypeStruct((tokens, 2 * width), jnp.bfloat16),
+            jax.ShapeDtypeStruct((blocks, rows, 2 * width), jnp.bfloat16),
+        ),
+        in_specs=[hbm, vmem, vmem],
+        out_specs=(vmem, hbm),
+        scratch_shapes=[
+            pltpu.VMEM((blocks, rows, 2 * width), jnp.bfloat16),
+            pltpu.VMEM(hidden.shape, jnp.bfloat16),
+            pltpu.SemaphoreType.DMA((64,)),
+            pltpu.SemaphoreType.DMA((64,)),
+            pltpu.SemaphoreType.DMA((2,)),
+        ],
+        compiler_params=pltpu.CompilerParams(
+            collective_id=0, has_side_effects=True, vmem_limit_bytes=48 << 20
+        ),
+        cost_estimate=pl.CostEstimate(
+            flops=2 * tokens * blocks * rows * 2 * width, bytes_accessed=22 << 20, transcendentals=0
+        ),
+    )(hidden, key_weight, value_weight)
+
+
+def attention_backward(hidden_rows, query_rows, grad_rows, slot_counts, key_rows, value_rows):
     slot_total, token_slots, width = hidden_rows.shape
     head_size = HD
-    kv_heads = key_full.shape[1] // head_size
+    kv_heads = key_rows.shape[1] // head_size
     flat_rows = hidden_rows.reshape(slot_total * token_slots, width)
-    key_rows = jnp.dot(flat_rows, key_full, preferred_element_type=jnp.float32).astype(jnp.bfloat16)
-    value_rows = jnp.dot(flat_rows, value_full, preferred_element_type=jnp.float32).astype(
-        jnp.bfloat16
-    )
     keys_split = key_rows.reshape(slot_total, token_slots, kv_heads, head_size)
     values_split = value_rows.reshape(slot_total, token_slots, kv_heads, head_size)
     query_split = query_rows.reshape(slot_total, token_slots, kv_heads, -1, head_size)
@@ -83,15 +286,13 @@
 
 def body(hidden, queries, out_grad, counts, send_peer, recv_from, key_weight, value_weight):
     width = key_weight.shape[1]
-    pair_full = lax.all_gather(
-        jnp.concatenate([key_weight, value_weight], axis=1), "fsdp", axis=0, tiled=True
-    )
-    key_full, value_full = pair_full[:, :width], pair_full[:, width:]
+    pair, w_blocks = gather_project(hidden, key_weight, value_weight)
+    pair_full = w_blocks.reshape(-1, 2 * width)
     group_count = lax.axis_size("dp")
     own_group = lax.axis_index("dp")
     chosen, placing, staying = block_plan(send_peer, recv_from, own_group, group_count)
     flat_rows, key_flat, value_flat = attention_backward(
-        hidden, queries, out_grad, counts.astype(jnp.float32), key_full, value_full
+        hidden, queries, out_grad, counts.astype(jnp.float32), pair[:, :width], pair[:, width:]
     )
     pair_delta = jnp.concatenate([key_flat, value_flat], axis=1)
     slots, tokens = hidden.shape[0], hidden.shape[1]

time: 370 us -> 326 us (0.88)
  waiting for transfers between devices: 229 us -> 162 us
  Pallas kernels: 0 us -> 46.4 us
  matrix products: 57.4 us -> 40.1 us
  local copies, waits for them, and re-layouts: 46.7 us -> 41.8 us
    all_gather x1 -> x0, waiting for transfers between devices: 66 us -> none  [body(): lax.all_gather(jnp.concatenate([key_weight, value_weight], axis=1), 'fsdp...]
    pallas_call x0 -> x1, Pallas kernels: none -> 46.4 us  [gather_project(): pl.pallas_call(gather_kernel, name='gather_project', out_shape=(jax.Shape...]
    dot_general x2 -> x0, matrix products: 14.7 us -> none  [the longest x1 7.76 us: attention_backward(): jnp.dot(flat_rows, value_full, preferred_element_type=jnp.float32)]
    unnamed x4 -> x3, waiting for transfers between devices: 90.7 us -> 90.8 us
    unnamed x22 -> x26, local copies, waits for them, and re-layouts: 21.4 us -> 21.4 us
  transfers between devices with their start and end apart: 4 -> 3, of which waited for: 4 -> 3; matrix products, arithmetic and copies ran while one was open for 10% -> 5% of each run, Pallas kernels for 0% -> 0%
where the time goes in v2:
time: 326 us; the launch traced here: 322 us
  waiting for transfers between devices  162 us (50%)
  Pallas kernels  46.4 us (14%)
  local copies, waits for them, and re-layouts  41.8 us (13%)
  matrix products  40.1 us (12%)
  between operations  14.3 us (4%)
  other arithmetic  13.5 us (4%)
  starting transfers between devices  3.57 us (1%)
    unnamed x3, waiting for transfers between devices  90.8 us
    psum x1, waiting for transfers between devices, body(): weight_grad = lax.psum(partial_rows, 'dp').astype(jnp.float32)  62.5 us
    pallas_call x1, Pallas kernels, gather_project(): pl.pallas_call(gather_kernel, name='gather_project', out_shape=(jax.Shape...  46.4 us
    unnamed x26, local copies, waits for them, and re-layouts  21.4 us
    dot_general x1, matrix products, body(): jnp.einsum('rk,dk->rd', settled, pair_full, preferred_element_type=jnp.fl...  11.3 us
    dot_general x1, matrix products, body(): jnp.einsum('rd,rk->dk', flat_rows, pair_delta, preferred_element_type=jnp...  10.8 us
    dot_general x1, matrix products, attention_backward(): jnp.einsum('sgrtu,stgrd->sugd', score_delta, query_split, preferred_eleme...  9.74 us
    all_to_all x1, waiting for transfers between devices, body(): lax.all_to_all(select_rows(chosen, pair_rows), 'dp', split_axis=0, concat...  9 us
  transfers between devices with their start and end apart: 3, of which 3 were waited for; matrix products, arithmetic and copies ran while one was open for 5% of the time, Pallas kernels for 0%

profile of v2, /device:TPU:1, one launch (start us, length us, event | category | flops | bytes accessed | tf_op | source)
XLA Modules:
  0.0 322.0 jit_solution(15529149966476747975)
XLA Ops:
  8.7 7.1 %reshape.120 = bf16[16,32,4,5,128]{4,3,2,1,0:T(8,128)(2,1)} reshape(bf16[16,32,2560]{2,1,0:T(8,128)(2,1)} %param.9) | data formatting | bytes 5242880 | tf_op jit(solution)/shard_map/reshape | solution.py:224
  15.8 4.8 %reshape.128 = f32[16,32,4,5,128]{4,3,2,1,0:T(8,128)} reshape(bf16[16,32,2560]{2,1,0:T(8,128)(2,1)S(1)} %copy-done.4) | data formatting | bytes 7864320 | tf_op jit(solution)/shard_map/convert_element_type | solution.py:244
  20.8 46.4 %gather_project.1 = (bf16[512,1024]{1,0:T(8,128)(2,1)S(1)}, bf16[16,320,1024]{2,1,0:T(8,128)(2,1)}) custom-call(bf16[16,32,5120]{2,1,0:T(8,128)(2,1)} %hidden.1, bf16[320,512]{1,0:T(8,128)(2,1)S(1)} %copy-done, bf16[320,512]{1,0:T(8,128)(2,1)S(1)} %copy-done.1), custom_call_target="tpu_custom_call" | custom-call | flops 5368709120 | bytes 23068672 | tf_op jit(solution)/shard_map/gather_project/pallas_call | solution.py:192
  68.3 8.2 %fusion.5 = bf16[16,32,4,5,128]{4,1,3,2,0:T(8,128)(2,1)S(1)} fusion(f32[16,32,4,5,128]{4,3,2,1,0:T(8,128)} %reshape.128, f32[16,32]{1,0:T(8,128)S(1)} %convert_divide_fusion), kind=kLoop, calls=%fused_computation.11 | loop fusion | flops 2621440 | bytes 7866368 | tf_op jit(solution)/shard_map/convert_element_type | solution.py:244
  76.5 3.6 %fusion.18 = f32[16,4,32,32,5]{3,2,4,1,0:T(8,128)S(1)} fusion(bf16[16,32,4,5,128]{4,3,2,1,0:T(8,128)(2,1)S(1)} %copy-done.2, bf16[16,32,4,128,1]{3,2,1,0,4:T(4,128)(2,1)S(1)} %bitcast.88), kind=kOutput, calls=%fused_computation.24 | convolution fusion | flops 83886080 | bytes 4456448 | tf_op jit(solution)/shard_map/stgrd,sugd->sgrtu/dot_general | solution.py:227
  80.3 2.5 fusion.63
  83.9 1.4 fusion.32
  85.3 2.4 fusion.1
  87.7 1.4 copy.68
  89.1 1.7 copy.37
  90.8 9.7 %fusion.33 = bf16[16,32,4,128]{3,1,2,0:T(8,128)(2,1)} fusion(bf16[16,32,4,5,128]{4,3,2,1,0:T(8,128)(2,1)} %reshape.120, bf16[16,32,4,5,128]{4,1,3,2,0:T(8,128)(2,1)S(1)} %fusion.5, f32[16,4,5,32]{3,2,1,0:T(8,128)S(1)} %copy.37, f32[16,4,5,32,32]{3,4,2,1,0:T(8,128)} %copy-done.3, f32[16,4,5,32]{3,2,1,0:T(8,128)} %copy-done.7, ...), kind=kOutput, calls=%fused_computation.34 | convolution fusion | flops 169672704 | bytes 7684096 | tf_op jit(solution)/shard_map/sgrtu,stgrd->sugd/dot_general | solution.py:254
  100.8 1.3 copy.39
  102.3 10.8 %convert_bitcast_fusion = bf16[5120,1024]{0,1:T(8,128)(2,1)} fusion(bf16[512,5120]{1,0:T(8,128)(2,1)} %bitcast.92, bf16[512,512]{1,0:T(8,128)(2,1)S(1)} %get-tuple-element.24, bf16[512,512]{1,0:T(8,128)(2,1)S(1)} %get-tuple-element.25), kind=kOutput, calls=%fused_computation.1 | convolution fusion | flops 5376049152 | bytes 16777216 | tf_op jit(solution)/shard_map/rd,rk->dk/dot_general | solution.py:304
  113.1 14.4 %copy.64 = bf16[5120,1024]{1,0:T(8,128)(2,1)} copy(bf16[5120,1024]{0,1:T(8,128)(2,1)} %convert_bitcast_fusion) | data formatting | bytes 20971520
  130.0 1.1 copy.43
  131.1 3.5 %all-to-all-start = ((bf16[8,32,1024]{2,1,0:T(8,128)(2,1)}), bf16[8,32,1024]{2,1,0:T(8,128)(2,1)S(1)}, u32[]{:S(2)}, u32[]{:S(2)}) async-start(bf16[8,32,1024]{2,1,0:T(8,128)(2,1)} %copy.43), calls=%async_computation | async-start | bytes 1048576 | tf_op jit(solution)/shard_map/all_to_all | solution.py:300
  134.7 9.0 %all-to-all-done = bf16[8,32,1024]{2,1,0:T(8,128)(2,1)S(1)} async-done(((bf16[8,32,1024]{2,1,0:T(8,128)(2,1)}), bf16[8,32,1024]{2,1,0:T(8,128)(2,1)S(1)}, u32[]{:S(2)}, u32[]{:S(2)}) %all-to-all-start) | async-done | bytes 524320 | tf_op jit(solution)/shard_map/all_to_all | solution.py:300
  144.8 90.8 %reduce-scatter.4.cloned.1.call-done = bf16[320,1024]{1,0:T(8,128)(2,1)} async-done(((bf16[5120,1024]{1,0:T(8,128)(2,1)}), bf16[320,1024]{1,0:T(8,128)(2,1)}) %reduce-scatter.4.cloned.1.call-update) | async-done | bytes 655376
  235.6 2.2 copy.65
  237.9 11.3 %convolution_convert_fusion = bf16[512,5120]{1,0:T(8,128)(2,1)} fusion(bf16[512,1024]{1,0:T(8,128)(2,1)S(1)} %bitcast.91, bf16[5120,1024]{1,0:T(8,128)(2,1)} %bitcast.93), kind=kOutput, calls=%fused_computation.2 | convolution fusion | flops 5371330560 | bytes 16777216 | tf_op jit(solution)/shard_map/rk,dk->rd/dot_general | solution.py:313
  249.2 62.5 %all-reduce.2.cloned.1.call-done = bf16[320,1024]{0,1:T(8,128)(2,1)} async-done(((bf16[320,1024]{0,1:T(8,128)(2,1)}), bf16[320,1024]{0,1:T(8,128)(2,1)}) %all-reduce.2.cloned.1.call-update) | async-done | bytes 655376 | tf_op jit(solution)/shard_map/psum | solution.py:317
  311.7 1.2 fusion.62
  312.9 1.1 copy.48
  314.0 1.1 copy.49
  (47 shorter events, 8.0 us)
Async XLA Ops:
  7.2 8.6 %copy-start.4 = (bf16[16,32,2560]{2,1,0:T(8,128)(2,1)S(1)}, bf16[16,32,2560]{2,1,0:T(8,128)(2,1)}, u32[]{:S(2)}) copy-start(bf16[16,32,2560]{2,1,0:T(8,128)(2,1)} %param.10) | copy-start | bytes 7864324
  7.2 228.4 %reduce-scatter.4.cloned.1.call-start = ((), (), s32[]{:S(2)}) async-start(), calls=%async_computation.3 | async-start | bytes 11141120
  15.8 5.0 %copy-start = (bf16[320,512]{1,0:T(8,128)(2,1)S(1)}, bf16[320,512]{1,0:T(8,128)(2,1)}, u32[]{:S(2)}) copy-start(bf16[320,512]{1,0:T(8,128)(2,1)} %kw.1) | copy-start | bytes 983044
  15.8 5.0 %copy-start.1 = (bf16[320,512]{1,0:T(8,128)(2,1)S(1)}, bf16[320,512]{1,0:T(8,128)(2,1)}, u32[]{:S(2)}) copy-start(bf16[320,512]{1,0:T(8,128)(2,1)} %vw.1) | copy-start | bytes 983044
  68.3 8.3 %copy-start.2 = (bf16[16,32,4,5,128]{4,3,2,1,0:T(8,128)(2,1)S(1)}, bf16[16,32,4,5,128]{4,3,2,1,0:T(8,128)(2,1)}, u32[]{:S(2)}) copy-start(bf16[16,32,4,5,128]{4,3,2,1,0:T(8,128)(2,1)} %reshape.120) | copy-start | bytes 7864324
  82.9 2.4 copy-start.3
  82.9 2.4 copy-start.7
  82.9 2.4 copy-start.5
  127.5 1.0 copy-start.6
  128.5 1.1 copy-start.9
  128.5 6.1 %copy-start.8 = (s32[16]{0:T(128)S(1)}, s32[16]{0:T(128)}, u32[]{:S(2)}) copy-start(s32[16]{0:T(128)} %param.13) | copy-start | bytes 196
  131.1 12.6 %all-to-all-start = ((bf16[8,32,1024]{2,1,0:T(8,128)(2,1)}), bf16[8,32,1024]{2,1,0:T(8,128)(2,1)S(1)}, u32[]{:S(2)}, u32[]{:S(2)}) async-start(bf16[8,32,1024]{2,1,0:T(8,128)(2,1)} %copy.43), calls=%async_computation | async-start | bytes 1048576 | tf_op jit(solution)/shard_map/all_to_all | solution.py:300
  134.6 177.1 %all-reduce.2.cloned.1.call-start = ((), (), s32[]{:S(2)}) async-start(), calls=%async_computation.2 | async-start | bytes 1572864 | tf_op jit(solution)/shard_map/psum | solution.py:317
Sparse Core Ops, SparseCore 0:
  127.6 107.9 reduce-scatter.3
  238.2 73.4 all-reduce.1
